TPU v7x, 128 devices: a whole 4x4x4 slice. The times are simulated.
128 devices in a mesh: enc: 8 (over x, core), own: 16 (over z, y).
Axes of the slice: x: 4, y: 4, z: 4, core: 2. Of those that a mesh axis runs over, the one named last changes fastest.
Arguments:
- features: bfloat16 [8192, 768], P(('enc', 'own')), may hold values from -6 to 6
- doc_cluster: int32 [8192], P(('enc', 'own')), may hold values from 0 to 63, as said below
- norm_gain: float32 [768], replicated, may hold values from 0.25 to 1.75
- w_in: bfloat16 [768, 3072], replicated, may hold values from -0.21875 to 0.21875
- b_in: float32 [3072], replicated, may hold values from -3 to 3
- w_out: bfloat16 [3072, 768], replicated, may hold values from -0.109375 to 0.109375
- members: bfloat16 [16, 8192, 768], P('own', 'enc'), may hold values from -6 to 6
- member_cluster: int32 [16, 8192], P('own', 'enc'), may hold values from 0 to 63, as said below
- cluster_range: int32 [64, 2], replicated, may hold values from 0 to 15, as said below
Outputs:
- embeddings: bfloat16 [8192, 768], P(('enc', 'own'))
- maxsim: float32 [8192], P(('enc', 'own'))
Inputs may be any that keep to these rules, and one draw needn't show every extreme that they name: `doc_cluster`: document k of a device's 64 belongs to a cluster whose range lies in owner group g = k mod (4), the owners 4 g to 4 g + 3. Of one device's documents at most 16 belong to clusters whose range holds a given owner; on every device some owner gets exactly 16. `cluster_range`: each cluster's range is an aligned run of 1, 2 or 4 owners inside an aligned group of four owners; every such group has a cluster that spans all four. `member_cluster`: A member's cluster has a range that holds the member's owner, and every owner in a cluster's range holds members of it.
All inputs are finite; a program needn't handle non-finite values.
Results may differ from a plain program's by a relative error of at most 0.0047.
Values may be sent and summed in bfloat16 or wider, within the bound.
A program may use at most 64 MiB of HBM per device.

v0:
```python
import math

import jax
import jax.numpy as jnp
from jax import lax
from jax.sharding import PartitionSpec as P

lowest_score = -1e30


def best_match(rows, labels, stored, stored_labels):
    count = rows.shape[0]
    total = stored.shape[0]
    width = rows.shape[1]
    row_block = 2048
    col_block = 1024
    scale = 1.0 / math.sqrt(width)
    stored_blocks = stored.reshape(total // col_block, col_block, width)
    label_blocks = stored_labels.reshape(total // col_block, col_block)

    def one_block(group):
        block, block_labels = group

        def advance(best, pieces):
            stock, stock_labels = pieces
            score = (
                lax.dot_general(
                    block, stock, (((1,), (1,)), ((), ())), preferred_element_type=jnp.float32
                )
                * scale
            )
            score = jnp.where(block_labels[:, None] == stock_labels[None, :], score, lowest_score)
            return (jnp.maximum(best, jnp.max(score, axis=1)), None)

        start = jnp.full((block.shape[0],), lowest_score, jnp.float32)
        best, unused = lax.scan(advance, start, (stored_blocks, label_blocks))
        return best

    result = lax.map(
        one_block,
        (
            rows.reshape(count // row_block, row_block, width),
            labels.reshape(count // row_block, row_block),
        ),
    )
    return result.reshape(count)


def shards(
    features, doc_cluster, norm_gain, w_in, b_in, w_out, members, member_cluster, cluster_range
):
    inputs = features.astype(jnp.float32)
    center = inputs - jnp.mean(inputs, axis=1, keepdims=True)
    spread = jnp.mean(center * center, axis=1, keepdims=True)
    normed = (center * lax.rsqrt(spread + 1e-05) * norm_gain).astype(jnp.bfloat16)
    hidden = jax.nn.gelu(
        jnp.dot(normed, w_in, preferred_element_type=jnp.float32) + b_in, approximate=True
    ).astype(jnp.bfloat16)
    output = inputs + jnp.dot(hidden, w_out, preferred_element_type=jnp.float32)
    embeddings = (
        output * lax.rsqrt(jnp.mean(output * output, axis=1, keepdims=True) + 1e-06)
    ).astype(jnp.bfloat16)
    owners_count = lax.axis_size("own")
    encoders = lax.axis_size("enc")
    docs_here = features.shape[0]
    width = features.shape[1]
    capacity = docs_here * 4 // owners_count
    clusters = cluster_range.shape[0]
    onehot = (doc_cluster[:, None] == jnp.arange(clusters, dtype=jnp.int32)[None, :]).astype(
        jnp.int32
    )
    lowest = jnp.sum(onehot * cluster_range[None, :, 0], axis=1)
    highest = jnp.sum(onehot * cluster_range[None, :, 1], axis=1)
    owner_index = jnp.arange(owners_count, dtype=jnp.int32)
    covers = (owner_index[None, :] >= lowest[:, None]) & (owner_index[None, :] <= highest[:, None])
    flags = covers.astype(jnp.int32)
    position = jnp.cumsum(flags, axis=0) - flags
    slots = owner_index[None, :] * capacity + position
    target = jnp.where(covers, slots, owners_count * capacity)
    sources = jnp.broadcast_to(jnp.arange(docs_here, dtype=jnp.int32)[:, None], covers.shape)
    root = (
        jnp.full((owners_count * capacity + 1,), -1, jnp.int32)
        .at[target.reshape(-1)]
        .set(sources.reshape(-1))[:-1]
    )
    filled = root >= 0
    safe = jnp.maximum(root, 0)
    send_rows = jnp.where(filled[:, None], embeddings[safe], jnp.zeros((), jnp.bfloat16)).reshape(
        owners_count, capacity, width
    )
    send_labels = jnp.where(filled, doc_cluster[safe], -1).reshape(owners_count, capacity)
    copies = jnp.broadcast_to(send_rows[None], (encoders, owners_count, capacity, width)).reshape(
        encoders * owners_count, capacity, width
    )
    copy_labels = jnp.broadcast_to(send_labels[None], (encoders, owners_count, capacity)).reshape(
        encoders * owners_count, capacity
    )
    stored = members.reshape(-1, width)
    stored_labels = member_cluster.reshape(-1)
    rows = lax.all_to_all(copies, ("enc", "own"), split_axis=0, concat_axis=0, tiled=True)
    labels = lax.all_to_all(copy_labels, ("enc", "own"), split_axis=0, concat_axis=0, tiled=True)
    senders = labels.shape[0]
    items = labels.shape[1]
    best = best_match(
        rows.reshape(senders * items, width), labels.reshape(-1), stored, stored_labels
    ).reshape(senders, items)
    replies = lax.all_to_all(best, ("enc", "own"), split_axis=0, concat_axis=0, tiled=True)
    returned = jnp.max(replies.reshape(encoders, owners_count, capacity), axis=0)
    picked = returned.reshape(-1)[jnp.where(covers, slots, 0)]
    maxsim = jnp.max(jnp.where(covers, picked, lowest_score), axis=1)
    return (embeddings, maxsim)


def solution(mesh):
    placed = (
        P(("enc", "own"), None),
        P(("enc", "own")),
        P(),
        P(),
        P(),
        P(),
        P("own", "enc", None),
        P("own", "enc"),
        P(),
    )
    return jax.shard_map(
        shards,
        mesh=mesh,
        in_specs=placed,
        out_specs=(P(("enc", "own"), None), P(("enc", "own"))),
        check_vma=False,
    )
```

profile of v0, /device:TPU:0, one launch (start us, length us, event | category | flops | bytes accessed | tf_op | source)
XLA Modules:
  0.0 111.5 jit_solution(13733925920474620636)
XLA Ops:
  0.7 0.8 slice_bitcast_fusion
  1.5 0.1 add.113
  1.6 0.8 select_reduce_fusion.3
  2.5 0.1 fusion.37
  2.6 0.1 reduce_window_sum.15
  2.7 0.1 reduce_window_sum.16
  2.8 0.1 and.24
  2.9 4.3 %scatter_custom_fusion = s32[257]{0:T(512)S(1)} fusion(s32[1024]{0:T(1024)S(1)} %bitcast.34, s32[1024]{0:T(1024)S(1)} %reshape.319, s32[]{:T(128)} %constant.46.clone.1), kind=kCustom, calls=%fused_computation.55 | custom fusion | bytes 1032 | tf_op jit(solution)/shard_map/scatter | solution.py:84
  7.2 0.1 ge.55
  7.3 1.9 %gather_fusion = s32[256]{0:T(256)S(1)} fusion(s32[64]{0:T(128)} %param.10, s32[1024]{0:T(1024)S(1)} %pad_clamp_fusion), kind=kCustom, calls=%fused_computation | custom fusion | bytes 3072 | tf_op jit(solution)/shard_map/gather | solution.py:91
  9.3 0.6 broadcast_in_dim.86
  9.9 11.1 %all-to-all-start = ((s32[128,1,16]{2,1,0:T(1,128)}), s32[128,1,16]{2,1,0:T(1,128)S(1)}, u32[]{:S(2)}, u32[]{:S(2)}) async-start(s32[128,1,16]{2,1,0:T(1,128)} %bitcast.3), calls=%async_computation | async-start | bytes 131072 | tf_op jit(solution)/shard_map/all_to_all | solution.py:101
  21.1 1.0 convert_reduce_fusion
  22.1 1.1 fusion.16
  23.2 5.9 %multiply_reduce_fusion = (f32[64]{0:T(128)S(1)}, f32[64,768]{1,0:T(8,128)S(1)}) fusion(bf16[3072,768]{1,0:T(8,128)(2,1)} %param.14, bf16[768,3072]{1,0:T(8,128)(2,1)} %param.12, f32[3072]{0:T(1024)} %param.13, bf16[64,768]{1,0:T(8,128)(2,1)} %param.9, f32[768]{0:T(1024)} %param.11, f32[64]{0:T(128)S(1)} %add_rsqrt_fusion.1, f32[64]{0:T(128)S(1)} %broadcast_multiply_fusion), kind=kOutput, calls=%fused_computation.31 | convolution fusion | flops 606388160 | bytes 9748224 | tf_op jit(solution)/shard_map/dot_general | solution.py:59
  29.2 0.1 multiply_convert_fusion
  29.3 1.2 %gather_fusion.1 = bf16[256,768]{1,0:T(8,128)(2,1)S(1)} fusion(bf16[64,768]{1,0:T(8,128)(2,1)S(1)} %multiply_convert_fusion, s32[1024]{0:T(1024)S(1)} %pad_clamp_fusion), kind=kCustom, calls=%fused_computation.1 | custom fusion | bytes 787456 | tf_op jit(solution)/shard_map/gather | solution.py:88
  30.5 0.1 broadcast_select_fusion
  30.6 2.0 %broadcast_in_dim.89 = bf16[8,16,16,768]{3,2,1,0:T(8,128)(2,1)} broadcast(bf16[16,16,768]{2,1,0:T(8,128)(2,1)S(1)} %broadcast_select_fusion), dimensions={1,2,3} | broadcast | bytes 3538944 | tf_op jit(solution)/shard_map/broadcast_in_dim | solution.py:92
  32.6 10.2 %all-to-all-start.1 = ((bf16[128,16,768]{2,1,0:T(8,128)(2,1)}), bf16[128,16,768]{2,1,0:T(8,128)(2,1)}, u32[]{:S(2)}, u32[]{:S(2)}) async-start(bf16[128,16,768]{2,1,0:T(8,128)(2,1)} %bitcast.31), calls=%async_computation.1 | async-start | bytes 6291456 | tf_op jit(solution)/shard_map/all_to_all | solution.py:100
  42.8 0.1 compare_select_fusion
  43.0 0.5 broadcast.235
  43.5 0.8 reduce.3
  44.3 0.1 eq.47
  44.4 38.3 %all-to-all-done.1 = bf16[128,16,768]{2,1,0:T(8,128)(2,1)} async-done(((bf16[128,16,768]{2,1,0:T(8,128)(2,1)}), bf16[128,16,768]{2,1,0:T(8,128)(2,1)}, u32[]{:S(2)}, u32[]{:S(2)}) %all-to-all-start.1) | async-done | bytes 3145760 | tf_op jit(solution)/shard_map/all_to_all | solution.py:100
  82.7 5.6 %select_reduce_fusion = f32[2048]{0:T(1024)S(1)} fusion(bf16[2048,768]{1,0:T(8,128)(2,1)} %bitcast.7, s32[2048]{0:T(1024)S(1)} %eq.47, s32[1024]{0:T(1024)S(1)} %bitcast.35, bf16[1,1024,768]{2,1,0:T(8,128)(2,1)S(1)} %copy-done), kind=kOutput, calls=%fused_computation.4 | convolution fusion | flops 3229612032 | bytes 4739072 | tf_op jit(solution)/shard_map/while/body/eval_jaxpr/while/body/eval_jaxpr/dot_general | solution.py:27
  88.3 0.7 max.21
  89.0 5.3 %all-to-all-start.2 = ((f32[128,1,16]{2,1,0:T(1,128)}), f32[128,1,16]{2,1,0:T(1,128)S(1)}, u32[]{:S(2)}, u32[]{:S(2)}) async-start(f32[128,1,16]{2,1,0:T(1,128)} %bitcast.9), calls=%async_computation.2 | async-start | bytes 131072 | tf_op jit(solution)/shard_map/all_to_all | solution.py:107
  94.3 9.5 %all-to-all-done.2 = f32[128,1,16]{2,1,0:T(1,128)S(1)} async-done(((f32[128,1,16]{2,1,0:T(1,128)}), f32[128,1,16]{2,1,0:T(1,128)S(1)}, u32[]{:S(2)}, u32[]{:S(2)}) %all-to-all-start.2) | async-done | bytes 8224 | tf_op jit(solution)/shard_map/all_to_all | solution.py:107
  103.8 0.1 reshape.290
  103.9 6.8 %gather_fusion.2 = f32[1024]{0:T(1024)S(1)} fusion(f32[256]{0:T(256)S(1)} %reshape.290, s32[1024]{0:T(1024)S(1)} %broadcast_clamp_fusion), kind=kCustom, calls=%fused_computation.2 | custom fusion | bytes 12288 | tf_op jit(solution)/shard_map/gather | solution.py:109
  110.8 0.7 select_reduce_fusion.1
  (25 shorter events, 0.4 us)
Async XLA Ops:
  0.6 82.1 %copy-start = (bf16[1,1024,768]{2,1,0:T(8,128)(2,1)S(1)}, bf16[1,1024,768]{2,1,0:T(8,128)(2,1)}, u32[]{:S(2)}) copy-start(bf16[1,1024,768]{2,1,0:T(8,128)(2,1)} %param.15) | copy-start | bytes 4718596
  9.9 20.6 %all-to-all-start = ((s32[128,1,16]{2,1,0:T(1,128)}), s32[128,1,16]{2,1,0:T(1,128)S(1)}, u32[]{:S(2)}, u32[]{:S(2)}) async-start(s32[128,1,16]{2,1,0:T(1,128)} %bitcast.3), calls=%async_computation | async-start | bytes 131072 | tf_op jit(solution)/shard_map/all_to_all | solution.py:101
  29.3 3.3 %copy-start.1 = (bf16[64,768]{1,0:T(8,128)(2,1)}, bf16[64,768]{1,0:T(8,128)(2,1)S(1)}, u32[]{:S(2)}) copy-start(bf16[64,768]{1,0:T(8,128)(2,1)S(1)} %multiply_convert_fusion) | copy-start | bytes 294916
  30.6 52.1 %copy-start.2 = (s32[1,1024]{1,0:T(1,128)S(1)}, s32[1,1024]{1,0:T(1,128)}, u32[]{:S(2)}) copy-start(s32[1,1024]{1,0:T(1,128)} %param.16) | copy-start | bytes 12292
  32.6 50.1 %all-to-all-start.1 = ((bf16[128,16,768]{2,1,0:T(8,128)(2,1)}), bf16[128,16,768]{2,1,0:T(8,128)(2,1)}, u32[]{:S(2)}, u32[]{:S(2)}) async-start(bf16[128,16,768]{2,1,0:T(8,128)(2,1)} %bitcast.31), calls=%async_computation.1 | async-start | bytes 6291456 | tf_op jit(solution)/shard_map/all_to_all | solution.py:100
  89.0 14.8 %all-to-all-start.2 = ((f32[128,1,16]{2,1,0:T(1,128)}), f32[128,1,16]{2,1,0:T(1,128)S(1)}, u32[]{:S(2)}, u32[]{:S(2)}) async-start(f32[128,1,16]{2,1,0:T(1,128)} %bitcast.9), calls=%async_computation.2 | async-start | bytes 131072 | tf_op jit(solution)/shard_map/all_to_all | solution.py:107
where the time goes:
time: 113 us; the launch traced here: 111 us
  waiting for transfers between devices  47.8 us (42%)
  starting transfers between devices  26.6 us (24%)
  local copies, waits for them, and re-layouts  19.7 us (17%)
  matrix products  11.5 us (10%)
  other arithmetic  4.99 us (4%)
    all_to_all x1, waiting for transfers between devices, shards(): lax.all_to_all(copies, ('enc', 'own'), split_axis=0, concat_axis=0, tiled...  38.3 us
    all_to_all x1, starting transfers between devices, shards(): lax.all_to_all(copy_labels, ('enc', 'own'), split_axis=0, concat_axis=0,...  11.1 us
    all_to_all x1, starting transfers between devices, shards(): lax.all_to_all(copies, ('enc', 'own'), split_axis=0, concat_axis=0, tiled...  10.2 us
    all_to_all x1, waiting for transfers between devices, shards(): lax.all_to_all(best, ('enc', 'own'), split_axis=0, concat_axis=0, tiled=T...  9.45 us
    gather x2, local copies, waits for them, and re-layouts, shards(): picked = returned.reshape(-1)[jnp.where(covers, slots, 0)]  6.9 us
    dot_general x1, matrix products, shards(): output = inputs + jnp.dot(hidden, w_out, preferred_element_type=jnp.float32)  5.92 us
    dot_general x1, matrix products, advance(): lax.dot_general(block, stock, (((1,), (1,)), ((), ())), preferred_element...  5.61 us
    all_to_all x1, starting transfers between devices, shards(): lax.all_to_all(best, ('enc', 'own'), split_axis=0, concat_axis=0, tiled=T...  5.28 us
  transfers between devices with their start and end apart: 3, of which 2 were waited for; matrix products, arithmetic and copies ran while one was open for 10% of the time, Pallas kernels for 0%

commit v1 on v0

v1 whole, which is shorter than its diff:
```python
import functools
import math

import jax
import jax.numpy as jnp
from jax import lax
from jax.experimental import pallas as pl
from jax.experimental.pallas import tpu as pltpu
from jax.sharding import PartitionSpec as P

MESH = pl.DeviceIdType.MESH
D = 768
HID = 3072
DOC = 64
MEM = 1024
CLUSTERS = 64
CHUNKS = 6
STEP = HID // CHUNKS
SCALE = 1.0 / math.sqrt(D)
LOWEST = -1e30 / SCALE
F32 = jnp.float32
BF16 = jnp.bfloat16


def iota(shape, dim):
    return lax.broadcasted_iota(jnp.int32, shape, dim)


def kernel(
    feat_h, dcl_h, gain_h, w1_h, bin_h, w2_h, mem_h, mcl_h, cr_h,
    emb_o, max_o,
    feat, dcl, gain, w1, bin_, w2, mem, mlab, cr,
    emb, sent, docs, memcol,
    lab_out, lab_z, lab_in, part, part_in, zmax, zin, row_out,
    load_sem, w_sem, out_sem,
    lz_s, lz_r, lp_s, lp_r, ml_s, ml_r, mm_s, mm_r,
    z_s, z_r, a_s, a_r, b_s, b_r, rp_s, rp_r, rz_s, rz_r,
):
    e = lax.axis_index("enc")
    o = lax.axis_index("own")
    x, c = e // 2, lax.rem(e, 2)
    z, y = o // 4, lax.rem(o, 4)
    a = x * (1 - c) + y * c
    b = y * (1 - c) + x * c

    def place(da, db, dz):
        pa, pb, pz = lax.rem(a + da, 4), lax.rem(b + db, 4), lax.rem(z + dz, 4)
        px = pa * (1 - c) + pb * c
        py = pb * (1 - c) + pa * c
        return (px * 2 + c, pz * 4 + py)

    other = (x * 2 + 1 - c, o)

    def remote(src, dst, ssem, rsem, where):
        return pltpu.make_async_remote_copy(
            src_ref=src, dst_ref=dst, send_sem=ssem, recv_sem=rsem,
            device_id=where, device_id_type=MESH,
        )

    def local(src, dst, sem):
        return pltpu.make_async_copy(src, dst, sem)

    small = [
        local(dcl_h, dcl, load_sem.at[0]),
        local(feat_h, feat, load_sem.at[1]),
        local(gain_h, gain, load_sem.at[2]),
        local(bin_h, bin_, load_sem.at[3]),
        local(cr_h, cr, load_sem.at[4]),
        local(mcl_h, mlab.at[0], load_sem.at[5]),
    ]
    for copy in small:
        copy.start()
    weights = []
    for j in range(CHUNKS):
        cols = pl.ds(j * STEP, STEP)
        weights.append((
            local(w1_h.at[:, cols], w1.at[:, cols], w_sem.at[0, j]),
            local(w2_h.at[cols], w2.at[cols], w_sem.at[1, j]),
        ))
        weights[-1][0].start()
        weights[-1][1].start()
    members = local(mem_h, mem.at[0], load_sem.at[6])

    plane = [(da, db) for db in range(4) for da in range(4) if (da, db) != (0, 0)]
    barrier = pltpu.get_barrier_semaphore()
    pl.semaphore_signal(barrier, inc=1, device_id=other, device_id_type=MESH)
    for d in (1, 2, 3):
        pl.semaphore_signal(barrier, inc=1, device_id=place(0, 0, d), device_id_type=MESH)
    for da, db in plane:
        pl.semaphore_signal(barrier, inc=1, device_id=place(da, db, 0), device_id_type=MESH)

    small[0].wait()
    k, lane = iota((DOC, 512), 0), iota((DOC, 512), 1)
    d, l = lane // 128, lane % 64
    hit = (k % 4 == (z + d) % 4) & (l // 16 == (4 - d) % 4) & (l % 16 == k // 4)
    spots = jnp.where(hit, 1.0, 0.0).astype(BF16)
    labels = jnp.broadcast_to(dcl[...].astype(F32), (8, DOC)).astype(BF16)
    spread = jnp.dot(labels, spots, preferred_element_type=F32)
    lab_z[0] = spread[:, :128]
    for d in (1, 2, 3):
        lab_out[d] = spread[:, d * 128 : (d + 1) * 128]

    pl.semaphore_wait(barrier, 4 + len(plane))
    lz = [remote(lab_out.at[d], lab_z.at[4 - d], lz_s.at[d], lz_r.at[4 - d], place(0, 0, d)) for d in (1, 2, 3)]
    for copy in lz:
        copy.start()
    small[5].wait()
    ml = remote(mlab.at[0], mlab.at[1], ml_s, ml_r, other)
    ml.start()

    small[1].wait()
    small[2].wait()
    r, k = iota((DOC, DOC), 0), iota((DOC, DOC), 1)
    order = jnp.where((k % 4 == (z + r // 16) % 4) & (k // 4 == r % 16), 1.0, 0.0).astype(BF16)
    inputs = jnp.dot(order, feat[...], preferred_element_type=F32)
    center = inputs - jnp.mean(inputs, axis=1, keepdims=True)
    spread = jnp.mean(center * center, axis=1, keepdims=True)
    normed = (center * lax.rsqrt(spread + 1e-05) * gain[...].reshape(1, D)).astype(BF16)
    small[3].wait()

    lp = [
        remote(lab_in.at[0, 0], lab_in.at[(4 - db) % 4, (4 - da) % 4],
               lp_s.at[db, da], lp_r.at[(4 - db) % 4, (4 - da) % 4], place(da, db, 0))
        for da, db in plane
    ]
    mm = remote(mem_h, mem.at[1], mm_s, mm_r, other)

    output = inputs
    for j in range(CHUNKS):
        weights[j][0].wait()
        pre = jnp.dot(normed, w1[:, j * STEP : (j + 1) * STEP], preferred_element_type=F32)
        hidden = jax.nn.gelu(pre + bin_[:, j * STEP : (j + 1) * STEP], approximate=True).astype(BF16)
        weights[j][1].wait()
        output = output + jnp.dot(hidden, w2[j * STEP : (j + 1) * STEP], preferred_element_type=F32)
        if j == 2:
            members.start()
            mm.start()
        if j == 3:
            for copy in lz:
                copy.wait_recv()
            lab_in[0, 0] = lab_z[0] + lab_z[1] + lab_z[2] + lab_z[3]
            for copy in lp:
                copy.start()
    found = (output * lax.rsqrt(jnp.mean(output * output, axis=1, keepdims=True) + 1e-06)).astype(BF16)
    sent[...] = found.reshape(4, 16, D)
    docs[0, 0, 0] = found[:16]

    zs = [remote(sent.at[d], docs.at[0, 0, 4 - d], z_s.at[d], z_r.at[4 - d], place(0, 0, d)) for d in (1, 2, 3)]
    for copy in zs:
        copy.start()

    k, r = iota((DOC, DOC), 0), iota((DOC, DOC), 1)
    back = jnp.where((k % 4 == (z + r // 16) % 4) & (k // 4 == r % 16), 1.0, 0.0).astype(BF16)
    emb[...] = jnp.dot(back, found, preferred_element_type=F32).astype(BF16)
    out = local(emb, emb_o, out_sem.at[0])
    out.start()

    A = {}
    B = {}

    def halves(dst, src, sem_s, sem_r, where, order):
        return {h: remote(src.at[pl.ds(2 * h, 2)], dst.at[pl.ds(2 * h, 2)], sem_s.at[h], sem_r.at[h], where) for h in order}

    A[3] = halves(docs.at[0, 3], docs.at[0, 0], a_s.at[3], a_r.at[3], place(1, 0, 0), (0, 1))
    A[1] = halves(docs.at[0, 1], docs.at[0, 0], a_s.at[1], a_r.at[1], place(3, 0, 0), (1, 0))
    A[2] = {
        0: remote(docs.at[0, 3, pl.ds(0, 2)], docs.at[0, 2, pl.ds(0, 2)], a_s.at[2, 0], a_r.at[2, 0], place(1, 0, 0)),
        1: remote(docs.at[0, 1, pl.ds(2, 2)], docs.at[0, 2, pl.ds(2, 2)], a_s.at[2, 1], a_r.at[2, 1], place(3, 0, 0)),
    }
    for da in range(4):
        B[da, 3] = halves(docs.at[3, da], docs.at[0, da], b_s.at[da, 3], b_r.at[da, 3], place(0, 1, 0), (0, 1))
        B[da, 1] = halves(docs.at[1, da], docs.at[0, da], b_s.at[da, 1], b_r.at[da, 1], place(0, 3, 0), (1, 0))
        B[da, 2] = {
            0: remote(docs.at[3, da, pl.ds(0, 2)], docs.at[2, da, pl.ds(0, 2)], b_s.at[da, 2, 0], b_r.at[da, 2, 0], place(0, 1, 0)),
            1: remote(docs.at[1, da, pl.ds(2, 2)], docs.at[2, da, pl.ds(2, 2)], b_s.at[da, 2, 1], b_r.at[da, 2, 1], place(0, 3, 0)),
        }

    for copy in zs:
        copy.wait_recv()
    A[3][0].start()
    A[1][1].start()
    A[3][1].start()
    A[1][0].start()

    def send_b(da):
        B[da, 3][0].start()
        B[da, 1][1].start()
        B[da, 3][1].start()
        B[da, 1][0].start()

    send_b(0)

    small[4].wait()
    ml.wait_recv()
    number = iota((1, CLUSTERS), 1)
    inside = (cr[0:1] <= o) & (o <= cr[1:2])
    named = jnp.where(inside, number, -1).astype(F32)
    square = iota((CLUSTERS, CLUSTERS), 0) == iota((CLUSTERS, CLUSTERS), 1)
    table = jnp.dot(
        jnp.where(square, named, 0.0).astype(BF16), jnp.ones((CLUSTERS, 128), BF16), preferred_element_type=F32
    ).astype(BF16)
    eye = iota((128, 128), 0) == iota((128, 128), 1)
    ones = jnp.ones((128, 128), BF16)
    for half in range(2):
        for i in range(8):
            row = mlab[half, i : i + 1, :].astype(F32)
            col = jnp.dot(jnp.where(eye, row, 0.0).astype(BF16), ones, preferred_element_type=F32)
            onehot = jnp.where(col[:, :CLUSTERS] == iota((128, CLUSTERS), 1).astype(F32), 1.0, 0.0).astype(BF16)
            memcol[pl.ds((half * 8 + i) * 128, 128), :] = jnp.dot(onehot, table, preferred_element_type=F32)
    for copy in lp:
        copy.wait_recv()

    A[3][0].wait_recv()
    A[2][0].start()
    A[1][1].wait_recv()
    A[2][1].start()
    A[3][1].wait_recv()
    A[1][0].wait_recv()
    send_b(3)
    send_b(1)
    A[2][0].wait_recv()
    A[2][1].wait_recv()
    send_b(2)

    def pass_on(da):
        B[da, 3][0].wait_recv()
        B[da, 2][0].start()
        B[da, 1][1].wait_recv()
        B[da, 2][1].start()

    low = iota((8, 128), 1) < 64
    copies = {}

    def match(db):
        block = docs[db].reshape(256, D)
        rows = [jnp.where(low, lab_in[db, 2 * h], lab_in[db, 2 * h + 1])[:1] for h in range(2)]
        best = [jnp.full((8, 128), LOWEST, F32)] * 2
        for i in range(4):
            stock = mem[i // 2, pl.ds((i % 2) * 512, 512), :]
            score = lax.dot_general(stock, block, (((1,), (1,)), ((), ())), preferred_element_type=F32)
            column = memcol[pl.ds(i * 512, 512), :]
            for h in range(2):
                kept = jnp.where(column == rows[h], score[:, h * 128 : (h + 1) * 128], LOWEST)
                best[h] = jnp.maximum(best[h], jnp.max(kept.reshape(64, 8, 128), axis=0))
        for h in range(2):
            part[db, h] = best[h]
        for da in range(4):
            if (da, db) == (0, 0):
                continue
            s, t = (4 - db) % 4, (4 - da) % 4
            copies[da, db] = remote(part.at[db, da // 2], part_in.at[s, t], rp_s.at[db, da], rp_r.at[s, t], place(da, db, 0))
            copies[da, db].start()

    pass_on(0)
    members.wait()
    mm.wait_recv()
    match(0)
    pass_on(3)
    pass_on(1)
    pass_on(2)
    for da in range(4):
        B[da, 3][1].wait_recv()
    match(3)
    for da in range(4):
        B[da, 1][0].wait_recv()
    match(1)
    for da in range(4):
        B[da, 2][0].wait_recv()
        B[da, 2][1].wait_recv()
    match(2)

    best = [part[0, 0], jnp.full((8, 128), LOWEST, F32)]
    for da, db in plane:
        s, t = (4 - db) % 4, (4 - da) % 4
        copies[da, db].wait_recv()
    for da, db in plane:
        s, t = (4 - db) % 4, (4 - da) % 4
        best[da % 2] = jnp.maximum(best[da % 2], part_in[s, t])
    merged = jnp.maximum(best[0], pltpu.roll(best[1], 64, axis=1))
    zmax[...] = merged
    rz = [remote(zmax, zin.at[4 - d], rz_s.at[d], rz_r.at[4 - d], place(0, 0, d)) for d in (1, 2, 3)]
    for copy in rz:
        copy.start()
    lane = iota((8, 128), 1)
    final = merged
    for copy in rz:
        copy.wait_recv()
    for d in (1, 2, 3):
        final = jnp.where(lane // 16 == d, zin[4 - d], final)
    final = jnp.max(final, axis=0, keepdims=True)[:, :DOC]
    l, k = iota((DOC, DOC), 0), iota((DOC, DOC), 1)
    column = jnp.max(jnp.where(l == k, final, LOWEST), axis=1, keepdims=True)
    takes = (k // 4 == l % 16) & (k % 4 == (z - l // 16 + 4) % 4)
    row = jnp.max(jnp.where(takes, column, LOWEST), axis=0, keepdims=True) * SCALE
    row_out[...] = row
    last = local(row_out, max_o, out_sem.at[1])
    last.start()
    last.wait()
    out.wait()

    for copy in (*lz, *lp, ml, mm, *zs, *copies.values(), *rz):
        copy.wait_send()
    for group in (*A.values(), *B.values()):
        for copy in group.values():
            copy.wait_send()


def step(features, doc_cluster, norm_gain, w_in, b_in, w_out, members, member_cluster, cluster_range):
    dma = pltpu.SemaphoreType.DMA
    anywhere = pl.BlockSpec(memory_space=pltpu.HBM)
    embeddings, best = pl.pallas_call(
        kernel,
        out_shape=(jax.ShapeDtypeStruct((DOC, D), BF16), jax.ShapeDtypeStruct((1, DOC), F32)),
        in_specs=[anywhere] * 9,
        out_specs=(anywhere, anywhere),
        scratch_shapes=[
            pltpu.VMEM((DOC, D), BF16),
            pltpu.VMEM((1, DOC), jnp.int32),
            pltpu.VMEM((D,), F32),
            pltpu.VMEM((D, HID), BF16),
            pltpu.VMEM((1, HID), F32),
            pltpu.VMEM((HID, D), BF16),
            pltpu.VMEM((2, MEM, D), BF16),
            pltpu.VMEM((2, 8, 128), jnp.int32),
            pltpu.VMEM((2, CLUSTERS), jnp.int32),
            pltpu.VMEM((DOC, D), BF16),
            pltpu.VMEM((4, 16, D), BF16),
            pltpu.VMEM((4, 4, 4, 16, D), BF16),
            pltpu.VMEM((2 * MEM, 128), F32),
            pltpu.VMEM((4, 8, 128), F32),
            pltpu.VMEM((4, 8, 128), F32),
            pltpu.VMEM((4, 4, 8, 128), F32),
            pltpu.VMEM((4, 2, 8, 128), F32),
            pltpu.VMEM((4, 4, 8, 128), F32),
            pltpu.VMEM((8, 128), F32),
            pltpu.VMEM((4, 8, 128), F32),
            pltpu.VMEM((1, DOC), F32),
            dma((7,)), dma((2, CHUNKS)), dma((2,)),
            dma((4,)), dma((4,)), dma((4, 4)), dma((4, 4)), dma, dma, dma, dma,
            dma((4,)), dma((4,)), dma((4, 2)), dma((4, 2)), dma((4, 4, 2)), dma((4, 4, 2)),
            dma((4, 4)), dma((4, 4)), dma((4,)), dma((4,)),
        ],
        compiler_params=pltpu.CompilerParams(
            collective_id=0, has_side_effects=True, vmem_limit_bytes=64 * 2**20
        ),
    )(
        features, doc_cluster.reshape(1, DOC), norm_gain, w_in, b_in.reshape(1, HID), w_out,
        members.reshape(MEM, D), member_cluster.reshape(8, 128), cluster_range.T,
    )
    return embeddings, best.reshape(DOC)


def solution(mesh):
    placed = (
        P(("enc", "own"), None), P(("enc", "own")), P(), P(), P(), P(),
        P("own", "enc", None), P("own", "enc"), P(),
    )
    return jax.shard_map(
        step, mesh=mesh, in_specs=placed, out_specs=(P(("enc", "own"), None), P(("enc", "own"))), check_vma=False
    )
```

time: 113 us -> 46.8 us (0.41); the launches traced: 111 us -> 46.7 us
  waiting for transfers between devices: 47.8 us -> 0 us
  Pallas kernels: 0 us -> 43.3 us
  starting transfers between devices: 26.6 us -> 0 us
  local copies, waits for them, and re-layouts: 19.7 us -> 2.73 us
  matrix products: 11.5 us -> 0 us
  other arithmetic: 4.99 us -> 0 us
    all_to_all x3 -> x0, waiting for transfers between devices: 47.8 us -> none  [the longest x1 38.3 us: shards(): lax.all_to_all(copies, ('enc', 'own'), split_axis=0, concat_axis=0, tiled...]
    pallas_call x0 -> x1, Pallas kernels: none -> 43.3 us  [step(): pl.pallas_call(kernel, out_shape=(jax.ShapeDtypeStruct((DOC, D), BF16), j...]
    all_to_all x3 -> x0, starting transfers between devices: 26.7 us -> none  [the longest x1 11.1 us: shards(): lax.all_to_all(copy_labels, ('enc', 'own'), split_axis=0, concat_axis=0,...]
    dot_general x2 -> x0, matrix products: 11.5 us -> none  [the longest x1 5.92 us: shards(): output = inputs + jnp.dot(hidden, w_out, preferred_element_type=jnp.float32)]
    gather x5 -> x0, local copies, waits for them, and re-layouts: 10.1 us -> none  [the longest x2 6.9 us: shards(): picked = returned.reshape(-1)[jnp.where(covers, slots, 0)]]
    scatter x1 -> x0, local copies, waits for them, and re-layouts: 4.3 us -> none  [shards(): root = jnp.full((owners_count * capacity + 1,), -1, jnp.int32).at[target....]
    reduce_sum x3 -> x0, other arithmetic: 2.93 us -> none  [the longest x1 1.09 us: shards(): spread = jnp.mean(center * center, axis=1, keepdims=True)]
    unnamed x6 -> x2, local copies, waits for them, and re-layouts: 0.02 us -> 2.73 us
  transfers between devices with their start and end apart: 3 -> 0, of which waited for: 2 -> 0; matrix products, arithmetic and copies ran while one was open for 10% -> 0% of each run, Pallas kernels for 0% -> 0%
where the time goes in v1:
time: 46.8 us; the launch traced here: 46.7 us
  Pallas kernels  43.3 us (93%)
  local copies, waits for them, and re-layouts  2.73 us (6%)
  between operations  0.64 us (1%)
    pallas_call x1, Pallas kernels, step(): pl.pallas_call(kernel, out_shape=(jax.ShapeDtypeStruct((DOC, D), BF16), j...  43.3 us
    unnamed x2, local copies, waits for them, and re-layouts  2.73 us

profile of v1, /device:TPU:0, one launch (start us, length us, event | category | flops | bytes accessed | tf_op | source)
XLA Modules:
  0.0 46.7 jit_solution(11849159828917629161)
XLA Ops:
  0.6 43.3 %shard_map.104 = (bf16[64,768]{1,0:T(8,128)(2,1)}, f32[1,64]{1,0:T(1,128)}) custom-call(bf16[64,768]{1,0:T(8,128)(2,1)} %feat_h.1, s32[1,64]{1,0:T(1,128)} %bitcast.10, f32[768]{0:T(1024)} %gain_h.1, bf16[768,3072]{1,0:T(8,128)(2,1)} %w1_h.1, f32[1,3072]{1,0:T(1,128)} %bitcast.7, bf16[3072,768]{1,0:T(8,128)(2,1)} %w2_h.1, bf16[1024,768]{1,0:T(8,128)(2,1)} %bitcast.6, ...), custom_call_target="tpu_custom_call" | custom-call | tf_op jit(solution)/shard_map/pallas_call | solution.py:311
  44.0 1.5 %copy.13 = bf16[64,768]{1,0:T(8,128)(2,1)} copy(bf16[64,768]{1,0:T(8,128)(2,1)} %get-tuple-element.8) | data formatting | bytes 196608
  45.5 1.2 %copy.14 = f32[64]{0:T(128)} copy(f32[64]{0:T(128)} %bitcast.11) | data formatting | bytes 512

commit v2 on v1

v2 whole, which is shorter than its diff:
```python
import functools
import math

import jax
import jax.numpy as jnp
from jax import lax
from jax.experimental import pallas as pl
from jax.experimental.pallas import tpu as pltpu
from jax.sharding import PartitionSpec as P

MESH = pl.DeviceIdType.MESH
D = 768
HID = 3072
DOC = 64
MEM = 1024
CLUSTERS = 64
CHUNKS = 6
WINDOW = 3
STEP = HID // CHUNKS
SCALE = 1.0 / math.sqrt(D)
LOWEST = -1e30 / SCALE
F32 = jnp.float32
BF16 = jnp.bfloat16


def iota(shape, dim):
    return lax.broadcasted_iota(jnp.int32, shape, dim)


def kernel(
    feat_h, dcl_h, gain_h, w1_h, bin_h, w2_h, mem_h, mcl_h, cr_h,
    emb_o, max_o,
    feat, dcl, gain, w1, bin_, w2, mem, mlab, cr,
    sent, docs, memcol,
    lab_out, lab_z, lab_in, part, part_in, most, most_in,
    load_sem, w_sem,
    lz_s, lz_r, lp_s, lp_r, ml_s, ml_r, mm_s, mm_r,
    z_s, z_r, b_s, b_r, rp_s, rp_r, rz_s, rz_r,
):
    e = lax.axis_index("enc")
    o = lax.axis_index("own")
    x, c = e // 2, lax.rem(e, 2)
    z, y = o // 4, lax.rem(o, 4)
    a = x * (1 - c) + y * c
    b = y * (1 - c) + x * c

    def place(da, db, dz):
        pa, pb, pz = lax.rem(a + da, 4), lax.rem(b + db, 4), lax.rem(z + dz, 4)
        px = pa * (1 - c) + pb * c
        py = pb * (1 - c) + pa * c
        return (px * 2 + c, pz * 4 + py)

    other = (x * 2 + 1 - c, o)

    def remote(src, dst, ssem, rsem, where):
        return pltpu.make_async_remote_copy(
            src_ref=src, dst_ref=dst, send_sem=ssem, recv_sem=rsem,
            device_id=where, device_id_type=MESH,
        )

    def local(src, dst, sem):
        return pltpu.make_async_copy(src, dst, sem)

    small = [
        local(dcl_h, dcl, load_sem.at[0]),
        local(feat_h, feat, load_sem.at[1]),
        local(gain_h, gain, load_sem.at[2]),
        local(bin_h, bin_, load_sem.at[3]),
        local(cr_h, cr, load_sem.at[4]),
        local(mcl_h, mlab.at[0], load_sem.at[5]),
    ]
    for copy in small:
        copy.start()
    weights = []
    for j in range(CHUNKS):
        cols = pl.ds(j * STEP, STEP)
        weights.append((
            local(w1_h.at[:, cols], w1.at[:, cols], w_sem.at[0, j]),
            local(w2_h.at[cols], w2.at[cols], w_sem.at[1, j]),
        ))
        if j < WINDOW:
            weights[-1][0].start()
            weights[-1][1].start()
    members = local(mem_h, mem.at[0], load_sem.at[6])

    near = [(da, dz) for da in (0, 2, 1, 3) for dz in (2, 1, 3, 0) if (da, dz) != (0, 0)]
    barrier = pltpu.get_barrier_semaphore()
    pl.semaphore_signal(barrier, inc=1, device_id=other, device_id_type=MESH)
    for db in (1, 2, 3):
        pl.semaphore_signal(barrier, inc=1, device_id=place(0, db, 0), device_id_type=MESH)
    for da, dz in near:
        pl.semaphore_signal(barrier, inc=1, device_id=place(da, 0, dz), device_id_type=MESH)

    small[0].wait()
    k, lane = iota((DOC, 512), 0), iota((DOC, 512), 1)
    d, l = lane // 128, lane % 64
    hit = (k % 4 == (z + d) % 4) & (l // 16 == (4 - d) % 4) & (l % 16 == k // 4)
    spots = jnp.where(hit, 1.0, 0.0).astype(BF16)
    labels = jnp.broadcast_to(dcl[...].astype(F32), (8, DOC)).astype(BF16)
    spread = jnp.dot(labels, spots, preferred_element_type=F32)
    lab_z[0, 0] = spread[:, :128]
    for d in range(4):
        lab_out[d] = spread[:, d * 128 : (d + 1) * 128]

    pl.semaphore_wait(barrier, 4 + len(near))
    lz = [
        remote(lab_out.at[dz], lab_z.at[-da % 4, -dz % 4], lz_s.at[da, dz], lz_r.at[-da % 4, -dz % 4], place(da, 0, dz))
        for da, dz in near
    ]
    for copy in lz:
        copy.start()
    small[5].wait()
    ml = remote(mlab.at[0], mlab.at[1], ml_s, ml_r, other)
    ml.start()

    small[1].wait()
    small[2].wait()
    r, k = iota((DOC, DOC), 0), iota((DOC, DOC), 1)
    order = jnp.where((k % 4 == (z + r // 16) % 4) & (k // 4 == r % 16), 1.0, 0.0).astype(BF16)
    inputs = jnp.dot(order, feat[...], preferred_element_type=F32)
    center = inputs - jnp.mean(inputs, axis=1, keepdims=True)
    spread = jnp.mean(center * center, axis=1, keepdims=True)
    normed = (center * lax.rsqrt(spread + 1e-05) * gain[...].reshape(1, D)).astype(BF16)
    small[3].wait()

    low = iota((8, 128), 1) < 64
    lp = [remote(lab_in.at[0], lab_in.at[4 - db], lp_s.at[db], lp_r.at[4 - db], place(0, db, 0)) for db in (1, 2, 3)]
    mm = remote(mem_h, mem.at[1], mm_s, mm_r, other)

    output = inputs
    for j in range(CHUNKS):
        weights[j][0].wait()
        pre = jnp.dot(normed, w1[:, j * STEP : (j + 1) * STEP], preferred_element_type=F32)
        hidden = jax.nn.gelu(pre + bin_[:, j * STEP : (j + 1) * STEP], approximate=True).astype(BF16)
        weights[j][1].wait()
        output = output + jnp.dot(hidden, w2[j * STEP : (j + 1) * STEP], preferred_element_type=F32)
        if j + WINDOW < CHUNKS:
            weights[j + WINDOW][0].start()
            weights[j + WINDOW][1].start()
        if j == 3:
            members.start()
            mm.start()
        if j == 5:
            for copy in lz:
                copy.wait_recv()
            sums = [lab_z[da, 0] + lab_z[da, 1] + lab_z[da, 2] + lab_z[da, 3] for da in range(4)]
            lab_in[0, 0] = jnp.where(low, sums[0], sums[1])
            lab_in[0, 1] = jnp.where(low, sums[2], sums[3])
            for copy in lp:
                copy.start()
    found = (output * lax.rsqrt(jnp.mean(output * output, axis=1, keepdims=True) + 1e-06)).astype(BF16)
    sent[...] = found.reshape(4, 16, D)
    docs[0, 0, 0] = found[:16]

    zs = {
        (-da % 4, -dz % 4): remote(
            sent.at[dz], docs.at[0, -da % 4, -dz % 4], z_s.at[da, dz], z_r.at[-da % 4, -dz % 4], place(da, 0, dz)
        )
        for da, dz in near
    }
    for copy in zs.values():
        copy.start()

    k, r = iota((DOC, DOC), 0), iota((DOC, DOC), 1)
    back = jnp.where((k % 4 == (z + r // 16) % 4) & (k // 4 == r % 16), 1.0, 0.0).astype(BF16)
    emb_o[...] = jnp.dot(back, found, preferred_element_type=F32).astype(BF16)

    B = {}

    def halves(dst, src, sem_s, sem_r, where, order):
        return {h: remote(src.at[pl.ds(2 * h, 2)], dst.at[pl.ds(2 * h, 2)], sem_s.at[h], sem_r.at[h], where) for h in order}

    for da in range(4):
        B[da, 3] = halves(docs.at[3, da], docs.at[0, da], b_s.at[da, 3], b_r.at[da, 3], place(0, 1, 0), (0, 1))
        B[da, 1] = halves(docs.at[1, da], docs.at[0, da], b_s.at[da, 1], b_r.at[da, 1], place(0, 3, 0), (1, 0))
        B[da, 2] = {
            0: remote(docs.at[3, da, pl.ds(0, 2)], docs.at[2, da, pl.ds(0, 2)], b_s.at[da, 2, 0], b_r.at[da, 2, 0], place(0, 1, 0)),
            1: remote(docs.at[1, da, pl.ds(2, 2)], docs.at[2, da, pl.ds(2, 2)], b_s.at[da, 2, 1], b_r.at[da, 2, 1], place(0, 3, 0)),
        }

    def send_b(da):
        for dz in range(4):
            if (da, dz) in zs:
                zs[da, dz].wait_recv()
        B[da, 3][0].start()
        B[da, 1][1].start()
        B[da, 3][1].start()
        B[da, 1][0].start()

    small[4].wait()
    ml.wait_recv()
    number = iota((1, CLUSTERS), 1)
    inside = (cr[0:1] <= o) & (o <= cr[1:2])
    named = jnp.where(inside, number, -1).astype(F32)
    square = iota((CLUSTERS, CLUSTERS), 0) == iota((CLUSTERS, CLUSTERS), 1)
    table = jnp.dot(
        jnp.where(square, named, 0.0).astype(BF16), jnp.ones((CLUSTERS, 128), BF16), preferred_element_type=F32
    ).astype(BF16)
    eye = iota((128, 128), 0) == iota((128, 128), 1)
    ones = jnp.ones((128, 128), BF16)
    for half in range(2):
        for i in range(8):
            row = mlab[half, i : i + 1, :].astype(F32)
            col = jnp.dot(jnp.where(eye, row, 0.0).astype(BF16), ones, preferred_element_type=F32)
            onehot = jnp.where(col[:, :CLUSTERS] == iota((128, CLUSTERS), 1).astype(F32), 1.0, 0.0).astype(BF16)
            memcol[pl.ds((half * 8 + i) * 128, 128), :] = jnp.dot(onehot, table, preferred_element_type=F32)
    for da in (0, 2, 1, 3):
        send_b(da)
    for copy in lp:
        copy.wait_recv()

    def pass_on(da):
        B[da, 3][0].wait_recv()
        B[da, 2][0].start()
        B[da, 1][1].wait_recv()
        B[da, 2][1].start()

    copies = []

    def match(db):
        block = docs[db].reshape(256, D)
        rows = [lab_in[db, h, :1] for h in range(2)]
        best = [jnp.full((8, 128), LOWEST, F32)] * 2
        for i in range(4):
            stock = mem[i // 2, pl.ds((i % 2) * 512, 512), :]
            score = lax.dot_general(stock, block, (((1,), (1,)), ((), ())), preferred_element_type=F32)
            column = memcol[pl.ds(i * 512, 512), :]
            for h in range(2):
                kept = jnp.where(column == rows[h], score[:, h * 128 : (h + 1) * 128], LOWEST)
                best[h] = jnp.maximum(best[h], jnp.max(kept.reshape(64, 8, 128), axis=0))
        for h in range(2):
            part[db, h] = best[h]
        if db:
            copies.append(remote(part.at[db], part_in.at[-db % 4], rp_s.at[db], rp_r.at[-db % 4], place(0, db, 0)))
            copies[-1].start()

    pass_on(0)
    members.wait()
    mm.wait_recv()
    match(0)
    for da in (2, 1, 3):
        pass_on(da)
    for da in range(4):
        B[da, 3][1].wait_recv()
    match(3)
    for da in range(4):
        B[da, 1][0].wait_recv()
    match(1)
    for da in range(4):
        B[da, 2][0].wait_recv()
        B[da, 2][1].wait_recv()
    match(2)

    for copy in copies:
        copy.wait_recv()
    most[...] = jnp.maximum(jnp.maximum(part[0], part_in[1]), jnp.maximum(part_in[2], part_in[3]))
    rz = [
        remote(most.at[da // 2], most_in.at[-da % 4, -dz % 4], rz_s.at[da, dz], rz_r.at[-da % 4, -dz % 4], place(da, 0, dz))
        for da, dz in near
    ]
    for copy in rz:
        copy.start()
    for copy in (*lz, *lp, ml, mm, *zs.values(), *copies):
        copy.wait_send()
    for group in B.values():
        for copy in group.values():
            copy.wait_send()
    most_in[0, 0] = most[0]
    for copy in rz:
        copy.wait_recv()
    quarter = iota((8, 128), 1) % 64 // 16
    sides = []
    for odd in range(2):
        side = jnp.full((8, 128), LOWEST, F32)
        for s in range(4):
            side = jnp.where(quarter == -s % 4, jnp.maximum(most_in[odd, s], most_in[odd + 2, s]), side)
        sides.append(side)
    final = jnp.maximum(sides[0], pltpu.roll(sides[1], 64, axis=1))
    final = jnp.max(final, axis=0, keepdims=True)[:, :DOC]
    l, k = iota((DOC, DOC), 0), iota((DOC, DOC), 1)
    column = jnp.max(jnp.where(l == k, final, LOWEST), axis=1, keepdims=True)
    takes = (k // 4 == l % 16) & (k % 4 == (z - l // 16 + 4) % 4)
    max_o[...] = jnp.max(jnp.where(takes, column, LOWEST), axis=0, keepdims=True) * SCALE
    for copy in rz:
        copy.wait_send()


def hand_on(embeddings, best, emb_o, max_o):
    emb_o[...] = embeddings[...]
    max_o[...] = best[...]


def step(features, doc_cluster, norm_gain, w_in, b_in, w_out, members, member_cluster, cluster_range):
    dma = pltpu.SemaphoreType.DMA
    anywhere = pl.BlockSpec(memory_space=pltpu.HBM)
    embeddings, best = pl.pallas_call(
        kernel,
        out_shape=(jax.ShapeDtypeStruct((DOC, D), BF16), jax.ShapeDtypeStruct((1, DOC), F32)),
        in_specs=[anywhere] * 9,
        out_specs=(pl.BlockSpec(memory_space=pltpu.VMEM), pl.BlockSpec(memory_space=pltpu.VMEM)),
        scratch_shapes=[
            pltpu.VMEM((DOC, D), BF16),
            pltpu.VMEM((1, DOC), jnp.int32),
            pltpu.VMEM((D,), F32),
            pltpu.VMEM((D, HID), BF16),
            pltpu.VMEM((1, HID), F32),
            pltpu.VMEM((HID, D), BF16),
            pltpu.VMEM((2, MEM, D), BF16),
            pltpu.VMEM((2, 8, 128), jnp.int32),
            pltpu.VMEM((2, CLUSTERS), jnp.int32),
            pltpu.VMEM((4, 16, D), BF16),
            pltpu.VMEM((4, 4, 4, 16, D), BF16),
            pltpu.VMEM((2 * MEM, 128), F32),
            pltpu.VMEM((4, 8, 128), F32),
            pltpu.VMEM((4, 4, 8, 128), F32),
            pltpu.VMEM((4, 2, 8, 128), F32),
            pltpu.VMEM((4, 2, 8, 128), F32),
            pltpu.VMEM((4, 2, 8, 128), F32),
            pltpu.VMEM((2, 8, 128), F32),
            pltpu.VMEM((4, 4, 8, 128), F32),
            dma((7,)), dma((2, CHUNKS)),
            dma((4, 4)), dma((4, 4)), dma((4,)), dma((4,)), dma, dma, dma, dma,
            dma((4, 4)), dma((4, 4)), dma((4, 4, 2)), dma((4, 4, 2)),
            dma((4,)), dma((4,)), dma((4, 4)), dma((4, 4)),
        ],
        compiler_params=pltpu.CompilerParams(
            collective_id=0, has_side_effects=True, vmem_limit_bytes=64 * 2**20
        ),
    )(
        features, doc_cluster.reshape(1, DOC), norm_gain, w_in, b_in.reshape(1, HID), w_out,
        members.reshape(MEM, D), member_cluster.reshape(8, 128), cluster_range.T,
    )
    embeddings, best = pl.pallas_call(
        hand_on,
        out_shape=(jax.ShapeDtypeStruct((DOC, D), BF16), jax.ShapeDtypeStruct((1, DOC), F32)),
        in_specs=[pl.BlockSpec(memory_space=pltpu.VMEM)] * 2,
        out_specs=(pl.BlockSpec(memory_space=pltpu.VMEM), pl.BlockSpec(memory_space=pltpu.VMEM)),
    )(embeddings, best)
    return embeddings, best.reshape(DOC)


def solution(mesh):
    placed = (
        P(("enc", "own"), None), P(("enc", "own")), P(), P(), P(), P(),
        P("own", "enc", None), P("own", "enc"), P(),
    )
    return jax.shard_map(
        step, mesh=mesh, in_specs=placed, out_specs=(P(("enc", "own"), None), P(("enc", "own"))), check_vma=False
    )
```

time: 46.8 us -> 42.3 us (0.904)
  local copies, waits for them, and re-layouts: 2.73 us -> 0 us
  Pallas kernels: 43.3 us -> 41.6 us
    pallas_call x1, Pallas kernels: 43.3 us -> 40 us  [step(): pl.pallas_call(kernel, out_shape=(jax.ShapeDtypeStruct((DOC, D), BF16), j...]
    unnamed x2 -> x0, local copies, waits for them, and re-layouts: 2.73 us -> none
    pallas_call x0 -> x1, Pallas kernels: none -> 1.55 us  [step(): pl.pallas_call(hand_on, out_shape=(jax.ShapeDtypeStruct((DOC, D), BF16),...]
where the time goes in v2:
time: 42.3 us; the launch traced here: 42.2 us
  Pallas kernels  41.6 us (98%)
  between operations  0.64 us (2%)
    pallas_call x1, Pallas kernels, step(): pl.pallas_call(kernel, out_shape=(jax.ShapeDtypeStruct((DOC, D), BF16), j...  40 us
    pallas_call x1, Pallas kernels, step(): pl.pallas_call(hand_on, out_shape=(jax.ShapeDtypeStruct((DOC, D), BF16),...  1.55 us

profile of v2, /device:TPU:0, one launch (start us, length us, event | category | flops | bytes accessed | tf_op | source)
XLA Modules:
  0.0 42.2 jit_solution(2363371850795311682)
XLA Ops:
  0.6 40.0 %shard_map.104 = (bf16[64,768]{1,0:T(8,128)(2,1)}, f32[1,64]{1,0:T(1,128)}) custom-call(bf16[64,768]{1,0:T(8,128)(2,1)} %feat_h.1, s32[1,64]{1,0:T(1,128)} %bitcast.10, f32[768]{0:T(1024)} %gain_h.1, bf16[768,3072]{1,0:T(8,128)(2,1)} %w1_h.1, f32[1,3072]{1,0:T(1,128)} %bitcast.7, bf16[3072,768]{1,0:T(8,128)(2,1)} %w2_h.1, bf16[1024,768]{1,0:T(8,128)(2,1)} %bitcast.6, ...), custom_call_target="tpu_custom_call" | custom-call | tf_op jit(solution)/shard_map/pallas_call | solution.py:296
  40.7 1.5 %shard_map.105 = (bf16[64,768]{1,0:T(8,128)(2,1)}, f32[1,64]{1,0:T(1,128)}) custom-call(bf16[64,768]{1,0:T(8,128)(2,1)} %get-tuple-element.6.embeddings, f32[1,64]{1,0:T(1,128)} %get-tuple-element.7.best), custom_call_target="tpu_custom_call" | custom-call | tf_op jit(solution)/shard_map/pallas_call | solution.py:333

commit v3 on v2

--- a/solution.py
+++ b/solution.py
@@ -102,16 +102,12 @@
     for d in range(4):
         lab_out[d] = spread[:, d * 128 : (d + 1) * 128]
 
-    pl.semaphore_wait(barrier, 4 + len(near))
     lz = [
         remote(lab_out.at[dz], lab_z.at[-da % 4, -dz % 4], lz_s.at[da, dz], lz_r.at[-da % 4, -dz % 4], place(da, 0, dz))
         for da, dz in near
     ]
-    for copy in lz:
-        copy.start()
     small[5].wait()
     ml = remote(mlab.at[0], mlab.at[1], ml_s, ml_r, other)
-    ml.start()
 
     small[1].wait()
     small[2].wait()
@@ -137,17 +133,14 @@
         if j + WINDOW < CHUNKS:
             weights[j + WINDOW][0].start()
             weights[j + WINDOW][1].start()
+        if j == 2:
+            pl.semaphore_wait(barrier, 4 + len(near))
+            for copy in lz:
+                copy.start()
+            ml.start()
         if j == 3:
             members.start()
             mm.start()
-        if j == 5:
-            for copy in lz:
-                copy.wait_recv()
-            sums = [lab_z[da, 0] + lab_z[da, 1] + lab_z[da, 2] + lab_z[da, 3] for da in range(4)]
-            lab_in[0, 0] = jnp.where(low, sums[0], sums[1])
-            lab_in[0, 1] = jnp.where(low, sums[2], sums[3])
-            for copy in lp:
-                copy.start()
     found = (output * lax.rsqrt(jnp.mean(output * output, axis=1, keepdims=True) + 1e-06)).astype(BF16)
     sent[...] = found.reshape(4, 16, D)
     docs[0, 0, 0] = found[:16]
@@ -184,8 +177,18 @@
                 zs[da, dz].wait_recv()
         B[da, 3][0].start()
         B[da, 1][1].start()
+
+    def send_rest(da):
         B[da, 3][1].start()
         B[da, 1][0].start()
+
+    for copy in lz:
+        copy.wait_recv()
+    sums = [lab_z[da, 0] + lab_z[da, 1] + lab_z[da, 2] + lab_z[da, 3] for da in range(4)]
+    lab_in[0, 0] = jnp.where(low, sums[0], sums[1])
+    lab_in[0, 1] = jnp.where(low, sums[2], sums[3])
+    for copy in lp:
+        copy.start()
 
     small[4].wait()
     ml.wait_recv()
@@ -204,16 +207,26 @@
             col = jnp.dot(jnp.where(eye, row, 0.0).astype(BF16), ones, preferred_element_type=F32)
             onehot = jnp.where(col[:, :CLUSTERS] == iota((128, CLUSTERS), 1).astype(F32), 1.0, 0.0).astype(BF16)
             memcol[pl.ds((half * 8 + i) * 128, 128), :] = jnp.dot(onehot, table, preferred_element_type=F32)
-    for da in (0, 2, 1, 3):
-        send_b(da)
-    for copy in lp:
-        copy.wait_recv()
-
     def pass_on(da):
         B[da, 3][0].wait_recv()
         B[da, 2][0].start()
         B[da, 1][1].wait_recv()
         B[da, 2][1].start()
+
+    send_b(0)
+    send_b(2)
+    send_b(1)
+    send_b(3)
+    send_rest(0)
+    send_rest(2)
+    send_rest(1)
+    send_rest(3)
+    pass_on(0)
+    pass_on(2)
+    pass_on(1)
+    pass_on(3)
+    for copy in lp:
+        copy.wait_recv()
 
     copies = []
 
@@ -234,12 +247,9 @@
             copies.append(remote(part.at[db], part_in.at[-db % 4], rp_s.at[db], rp_r.at[-db % 4], place(0, db, 0)))
             copies[-1].start()
 
-    pass_on(0)
     members.wait()
     mm.wait_recv()
     match(0)
-    for da in (2, 1, 3):
-        pass_on(da)
     for da in range(4):
         B[da, 3][1].wait_recv()
     match(3)

time: 42.3 us -> 40.2 us (0.950)
  Pallas kernels: 41.6 us -> 39.4 us
    pallas_call x1, Pallas kernels: 40 us -> 37.9 us  [step(): pl.pallas_call(kernel, out_shape=(jax.ShapeDtypeStruct((DOC, D), BF16), j...]
where the time goes in v3:
time: 40.2 us; the launch traced here: 40.1 us
  Pallas kernels  39.4 us (98%)
  between operations  0.64 us (2%)
    pallas_call x1, Pallas kernels, step(): pl.pallas_call(kernel, out_shape=(jax.ShapeDtypeStruct((DOC, D), BF16), j...  37.9 us
    pallas_call x1, Pallas kernels, step(): pl.pallas_call(hand_on, out_shape=(jax.ShapeDtypeStruct((DOC, D), BF16),...  1.55 us

profile of v3, /device:TPU:0, one launch (start us, length us, event | category | flops | bytes accessed | tf_op | source)
XLA Modules:
  0.0 40.1 jit_solution(8482720013479648090)
XLA Ops:
  0.6 37.9 %shard_map.104 = (bf16[64,768]{1,0:T(8,128)(2,1)}, f32[1,64]{1,0:T(1,128)}) custom-call(bf16[64,768]{1,0:T(8,128)(2,1)} %feat_h.1, s32[1,64]{1,0:T(1,128)} %bitcast.10, f32[768]{0:T(1024)} %gain_h.1, bf16[768,3072]{1,0:T(8,128)(2,1)} %w1_h.1, f32[1,3072]{1,0:T(1,128)} %bitcast.7, bf16[3072,768]{1,0:T(8,128)(2,1)} %w2_h.1, bf16[1024,768]{1,0:T(8,128)(2,1)} %bitcast.6, ...), custom_call_target="tpu_custom_call" | custom-call | tf_op jit(solution)/shard_map/pallas_call | solution.py:306
  38.5 1.5 %shard_map.105 = (bf16[64,768]{1,0:T(8,128)(2,1)}, f32[1,64]{1,0:T(1,128)}) custom-call(bf16[64,768]{1,0:T(8,128)(2,1)} %get-tuple-element.6.embeddings, f32[1,64]{1,0:T(1,128)} %get-tuple-element.7.best), custom_call_target="tpu_custom_call" | custom-call | tf_op jit(solution)/shard_map/pallas_call | solution.py:343

commit v4 on v3

--- a/solution.py
+++ b/solution.py
@@ -32,10 +32,10 @@
     emb_o, max_o,
     feat, dcl, gain, w1, bin_, w2, mem, mlab, cr,
     sent, docs, memcol,
-    lab_out, lab_z, lab_in, part, part_in, most, most_in,
+    lab_out, lab_z, lab_in, part, part_in,
     load_sem, w_sem,
     lz_s, lz_r, lp_s, lp_r, ml_s, ml_r, mm_s, mm_r,
-    z_s, z_r, b_s, b_r, rp_s, rp_r, rz_s, rz_r,
+    z_s, z_r, b_s, b_r, rp_s, rp_r,
 ):
     e = lax.axis_index("enc")
     o = lax.axis_index("own")
@@ -86,10 +86,25 @@
     near = [(da, dz) for da in (0, 2, 1, 3) for dz in (2, 1, 3, 0) if (da, dz) != (0, 0)]
     barrier = pltpu.get_barrier_semaphore()
     pl.semaphore_signal(barrier, inc=1, device_id=other, device_id_type=MESH)
-    for db in (1, 2, 3):
-        pl.semaphore_signal(barrier, inc=1, device_id=place(0, db, 0), device_id_type=MESH)
-    for da, dz in near:
-        pl.semaphore_signal(barrier, inc=1, device_id=place(da, 0, dz), device_id_type=MESH)
+    for da in range(4):
+        for db in range(4):
+            for dz in range(4):
+                if da or db or dz:
+                    pl.semaphore_signal(barrier, inc=1, device_id=place(da, db, dz), device_id_type=MESH)
+
+    small[1].wait()
+    small[2].wait()
+    r, k = iota((DOC, DOC), 0), iota((DOC, DOC), 1)
+    order = jnp.where((k % 4 == (z + r // 16) % 4) & (k // 4 == r % 16), 1.0, 0.0).astype(BF16)
+    inputs = jnp.dot(order, feat[...], preferred_element_type=F32)
+    center = inputs - jnp.mean(inputs, axis=1, keepdims=True)
+    spread = jnp.mean(center * center, axis=1, keepdims=True)
+    normed = (center * lax.rsqrt(spread + 1e-05) * gain[...].reshape(1, D)).astype(BF16)
+    small[3].wait()
+
+    low = iota((8, 128), 1) < 64
+    lp = [remote(lab_in.at[0], lab_in.at[4 - db], lp_s.at[db], lp_r.at[4 - db], place(0, db, 0)) for db in (1, 2, 3)]
+    mm = remote(mem_h, mem.at[1], mm_s, mm_r, other)
 
     small[0].wait()
     k, lane = iota((DOC, 512), 0), iota((DOC, 512), 1)
@@ -108,20 +123,6 @@
     ]
     small[5].wait()
     ml = remote(mlab.at[0], mlab.at[1], ml_s, ml_r, other)
-
-    small[1].wait()
-    small[2].wait()
-    r, k = iota((DOC, DOC), 0), iota((DOC, DOC), 1)
-    order = jnp.where((k % 4 == (z + r // 16) % 4) & (k // 4 == r % 16), 1.0, 0.0).astype(BF16)
-    inputs = jnp.dot(order, feat[...], preferred_element_type=F32)
-    center = inputs - jnp.mean(inputs, axis=1, keepdims=True)
-    spread = jnp.mean(center * center, axis=1, keepdims=True)
-    normed = (center * lax.rsqrt(spread + 1e-05) * gain[...].reshape(1, D)).astype(BF16)
-    small[3].wait()
-
-    low = iota((8, 128), 1) < 64
-    lp = [remote(lab_in.at[0], lab_in.at[4 - db], lp_s.at[db], lp_r.at[4 - db], place(0, db, 0)) for db in (1, 2, 3)]
-    mm = remote(mem_h, mem.at[1], mm_s, mm_r, other)
 
     output = inputs
     for j in range(CHUNKS):
@@ -134,7 +135,7 @@
             weights[j + WINDOW][0].start()
             weights[j + WINDOW][1].start()
         if j == 2:
-            pl.semaphore_wait(barrier, 4 + len(near))
+            pl.semaphore_wait(barrier, 64)
             for copy in lz:
                 copy.start()
             ml.start()
@@ -242,10 +243,15 @@
                 kept = jnp.where(column == rows[h], score[:, h * 128 : (h + 1) * 128], LOWEST)
                 best[h] = jnp.maximum(best[h], jnp.max(kept.reshape(64, 8, 128), axis=0))
         for h in range(2):
-            part[db, h] = best[h]
-        if db:
-            copies.append(remote(part.at[db], part_in.at[-db % 4], rp_s.at[db], rp_r.at[-db % 4], place(0, db, 0)))
-            copies[-1].start()
+            part[db, h] = jnp.max(best[h], axis=0, keepdims=True)
+        for da in (2, 1, 3, 0):
+            for dz in (2, 1, 3, 0):
+                if da or db or dz:
+                    copies.append(remote(
+                        part.at[db, da // 2], part_in.at[-db % 4, -da % 4, -dz % 4],
+                        rp_s.at[db, da, dz], rp_r.at[-db % 4, -da % 4, -dz % 4], place(da, db, dz),
+                    ))
+                    copies[-1].start()
 
     members.wait()
     mm.wait_recv()
@@ -261,37 +267,30 @@
         B[da, 2][1].wait_recv()
     match(2)
 
-    for copy in copies:
-        copy.wait_recv()
-    most[...] = jnp.maximum(jnp.maximum(part[0], part_in[1]), jnp.maximum(part_in[2], part_in[3]))
-    rz = [
-        remote(most.at[da // 2], most_in.at[-da % 4, -dz % 4], rz_s.at[da, dz], rz_r.at[-da % 4, -dz % 4], place(da, 0, dz))
-        for da, dz in near
-    ]
-    for copy in rz:
-        copy.start()
-    for copy in (*lz, *lp, ml, mm, *zs.values(), *copies):
+    part_in[0, 0, 0] = part[0, 0]
+    for copy in (*lz, *lp, ml, mm, *zs.values()):
         copy.wait_send()
     for group in B.values():
         for copy in group.values():
             copy.wait_send()
-    most_in[0, 0] = most[0]
-    for copy in rz:
+    for copy in copies:
         copy.wait_recv()
-    quarter = iota((8, 128), 1) % 64 // 16
+    quarter = iota((1, 128), 1) % 64 // 16
     sides = []
     for odd in range(2):
-        side = jnp.full((8, 128), LOWEST, F32)
+        side = jnp.full((1, 128), LOWEST, F32)
         for s in range(4):
-            side = jnp.where(quarter == -s % 4, jnp.maximum(most_in[odd, s], most_in[odd + 2, s]), side)
+            most = part_in[0, odd, s]
+            for q in range(1, 8):
+                most = jnp.maximum(most, part_in[q // 2, odd + q % 2 * 2, s])
+            side = jnp.where(quarter == -s % 4, most, side)
         sides.append(side)
-    final = jnp.maximum(sides[0], pltpu.roll(sides[1], 64, axis=1))
-    final = jnp.max(final, axis=0, keepdims=True)[:, :DOC]
+    final = jnp.maximum(sides[0], pltpu.roll(sides[1], 64, axis=1))[:, :DOC]
     l, k = iota((DOC, DOC), 0), iota((DOC, DOC), 1)
     column = jnp.max(jnp.where(l == k, final, LOWEST), axis=1, keepdims=True)
     takes = (k // 4 == l % 16) & (k % 4 == (z - l // 16 + 4) % 4)
     max_o[...] = jnp.max(jnp.where(takes, column, LOWEST), axis=0, keepdims=True) * SCALE
-    for copy in rz:
+    for copy in copies:
         copy.wait_send()
 
 
@@ -324,14 +323,12 @@
             pltpu.VMEM((4, 8, 128), F32),
             pltpu.VMEM((4, 4, 8, 128), F32),
             pltpu.VMEM((4, 2, 8, 128), F32),
-            pltpu.VMEM((4, 2, 8, 128), F32),
-            pltpu.VMEM((4, 2, 8, 128), F32),
-            pltpu.VMEM((2, 8, 128), F32),
-            pltpu.VMEM((4, 4, 8, 128), F32),
+            pltpu.VMEM((4, 2, 1, 128), F32),
+            pltpu.VMEM((4, 4, 4, 1, 128), F32),
             dma((7,)), dma((2, CHUNKS)),
             dma((4, 4)), dma((4, 4)), dma((4,)), dma((4,)), dma, dma, dma, dma,
             dma((4, 4)), dma((4, 4)), dma((4, 4, 2)), dma((4, 4, 2)),
-            dma((4,)), dma((4,)), dma((4, 4)), dma((4, 4)),
+            dma((4, 4, 4)), dma((4, 4, 4)),
         ],
         compiler_params=pltpu.CompilerParams(
             collective_id=0, has_side_effects=True, vmem_limit_bytes=64 * 2**20

time: 40.2 us -> 39 us (0.970)
  Pallas kernels: 39.4 us -> 38.2 us
    pallas_call x1, Pallas kernels: 37.9 us -> 36.7 us  [step(): pl.pallas_call(kernel, out_shape=(jax.ShapeDtypeStruct((DOC, D), BF16), j...]
where the time goes in v4:
time: 39 us; the launch traced here: 38.9 us
  Pallas kernels  38.2 us (98%)
  between operations  0.64 us (2%)
    pallas_call x1, Pallas kernels, step(): pl.pallas_call(kernel, out_shape=(jax.ShapeDtypeStruct((DOC, D), BF16), j...  36.7 us
    pallas_call x1, Pallas kernels, step(): pl.pallas_call(hand_on, out_shape=(jax.ShapeDtypeStruct((DOC, D), BF16),...  1.55 us

profile of v4, /device:TPU:0, one launch (start us, length us, event | category | flops | bytes accessed | tf_op | source)
XLA Modules:
  0.0 38.9 jit_solution(1193758969547243390)
XLA Ops:
  0.6 36.7 %shard_map.104 = (bf16[64,768]{1,0:T(8,128)(2,1)}, f32[1,64]{1,0:T(1,128)}) custom-call(bf16[64,768]{1,0:T(8,128)(2,1)} %feat_h.1, s32[1,64]{1,0:T(1,128)} %bitcast.10, f32[768]{0:T(1024)} %gain_h.1, bf16[768,3072]{1,0:T(8,128)(2,1)} %w1_h.1, f32[1,3072]{1,0:T(1,128)} %bitcast.7, bf16[3072,768]{1,0:T(8,128)(2,1)} %w2_h.1, bf16[1024,768]{1,0:T(8,128)(2,1)} %bitcast.6, ...), custom_call_target="tpu_custom_call" | custom-call | tf_op jit(solution)/shard_map/pallas_call | solution.py:305
  37.3 1.5 %shard_map.105 = (bf16[64,768]{1,0:T(8,128)(2,1)}, f32[1,64]{1,0:T(1,128)}) custom-call(bf16[64,768]{1,0:T(8,128)(2,1)} %get-tuple-element.6.embeddings, f32[1,64]{1,0:T(1,128)} %get-tuple-element.7.best), custom_call_target="tpu_custom_call" | custom-call | tf_op jit(solution)/shard_map/pallas_call | solution.py:340

commit v5 on v4

--- a/solution.py
+++ b/solution.py
@@ -83,7 +83,7 @@
             weights[-1][1].start()
     members = local(mem_h, mem.at[0], load_sem.at[6])
 
-    near = [(da, dz) for da in (0, 2, 1, 3) for dz in (2, 1, 3, 0) if (da, dz) != (0, 0)]
+    near = [(da, dz) for da in (0, 1, 3, 2) for dz in (2, 1, 3, 0) if (da, dz) != (0, 0)]
     barrier = pltpu.get_barrier_semaphore()
     pl.semaphore_signal(barrier, inc=1, device_id=other, device_id_type=MESH)
     for da in range(4):
@@ -215,9 +215,9 @@
         B[da, 2][1].start()
 
     send_b(0)
-    send_b(2)
     send_b(1)
     send_b(3)
+    send_b(2)
     send_rest(0)
     send_rest(2)
     send_rest(1)

time: 39 us -> 39 us (level)
  no operation moved by 1% of the time
where the time goes in v5:
time: 39 us; the launch traced here: 38.9 us
  Pallas kernels  38.2 us (98%)
  between operations  0.64 us (2%)
    pallas_call x1, Pallas kernels, step(): pl.pallas_call(kernel, out_shape=(jax.ShapeDtypeStruct((DOC, D), BF16), j...  36.7 us
    pallas_call x1, Pallas kernels, step(): pl.pallas_call(hand_on, out_shape=(jax.ShapeDtypeStruct((DOC, D), BF16),...  1.55 us

profile of v5, /device:TPU:0, one launch (start us, length us, event | category | flops | bytes accessed | tf_op | source)
XLA Modules:
  0.0 38.9 jit_solution(16831875602166820969)
XLA Ops:
  0.6 36.7 %shard_map.104 = (bf16[64,768]{1,0:T(8,128)(2,1)}, f32[1,64]{1,0:T(1,128)}) custom-call(bf16[64,768]{1,0:T(8,128)(2,1)} %feat_h.1, s32[1,64]{1,0:T(1,128)} %bitcast.10, f32[768]{0:T(1024)} %gain_h.1, bf16[768,3072]{1,0:T(8,128)(2,1)} %w1_h.1, f32[1,3072]{1,0:T(1,128)} %bitcast.7, bf16[3072,768]{1,0:T(8,128)(2,1)} %w2_h.1, bf16[1024,768]{1,0:T(8,128)(2,1)} %bitcast.6, ...), custom_call_target="tpu_custom_call" | custom-call | tf_op jit(solution)/shard_map/pallas_call | solution.py:305
  37.3 1.5 %shard_map.105 = (bf16[64,768]{1,0:T(8,128)(2,1)}, f32[1,64]{1,0:T(1,128)}) custom-call(bf16[64,768]{1,0:T(8,128)(2,1)} %get-tuple-element.6.embeddings, f32[1,64]{1,0:T(1,128)} %get-tuple-element.7.best), custom_call_target="tpu_custom_call" | custom-call | tf_op jit(solution)/shard_map/pallas_call | solution.py:340
